TPU v7x, 32 devices: a whole 2x2x4 slice. The times are simulated.
32 devices in a mesh: cube: 32 (over z, y, x, core).
Axes of the slice: x: 2, y: 2, z: 4, core: 2. Of those that a mesh axis runs over, the one named last changes fastest.
Arguments:
- vectors: bfloat16 [131072, 768], P('cube'), may hold values from -40 to 40
- child_labels: int32 [2, 131072], P(None, 'cube'), may hold values from 0 to 1, as said below
Outputs:
- held: bfloat16 [229376, 768], P('cube')
- margin_one: float32 [196608], P('cube')
- margin_two: float32 [229376], P('cube')
- centroids: float32 [6, 768], replicated
Inputs may be any that keep to these rules, and one draw needn't show every extreme that they name: `child_labels`: per device, the vectors leaving at the first level number from 1024 to 2048, and 2048 on some device in every draw. `child_labels`: per device, the second-level leavers among its vectors that stay at the first level number at most 512, and among the vectors it sends away at the first level at most 512; in every draw some device holds 512 second-level leavers of each kind (its own stayers and those received at the first level), so its second-level send buffer is full.
All inputs are finite; a program needn't handle non-finite values.
Results may differ from a plain program's by a relative error of at most 0.0011.
Values may be sent and summed in bfloat16 or wider, within the bound.
No kernel may reach another device: no remote copies, remote signals or barrier semaphores. Data moves between devices by JAX's collectives and lax.ppermute only.
A program may use at most 128 MiB of HBM per device.

v0:
```python
import jax
import jax.numpy as jnp
from jax import lax
from jax.sharding import PartitionSpec as P


def from_partner(shard, axis, stride):
    return lax.ppermute(shard, axis, [(i, i ^ 1 << stride) for i in range(lax.axis_size(axis))])


def shortened(shard):

    def short(part):
        return part.astype(jnp.bfloat16) if part.dtype == jnp.float32 else part

    return jax.tree.map(short, shard)


def compact(mask, rows, cap, fill):
    place = jnp.cumsum(mask.astype(jnp.int32)) - 1
    index = jnp.where(mask, place, cap)
    base = jnp.full((cap + 1,) + rows.shape[1:], fill, rows.dtype)
    return base.at[index].set(rows)[:cap]


def split_margin(held_rows, live, pair, width):
    scores = jnp.dot(held_rows, pair.astype(jnp.bfloat16).T, preferred_element_type=jnp.float32)
    offset = 0.5 * (jnp.sum(pair[1] * pair[1]) - jnp.sum(pair[0] * pair[0]))
    return jnp.where(live, (scores[:, 1] - scores[:, 0] - offset) / width, jnp.float32(0.0))


def local(vectors, child_labels):
    ways = lax.axis_size("cube")
    levels = ways.bit_length() - 1
    top_bit = levels - 1
    next_bit = levels - 2
    here = lax.axis_index("cube")
    bit_one = here >> top_bit & 1
    bit_two = here >> next_bit & 1
    rows, width = vectors.shape
    cap_one = rows // 2
    cap_two = rows // 4
    first = child_labels[0]
    later = child_labels[1]
    leave = first != bit_one
    stay = jnp.logical_not(leave)
    send_rows = compact(leave, vectors, cap_one, 0)
    send_tags = compact(leave, later, cap_one, -1)
    got_rows, got_tags = from_partner((send_rows, send_tags), "cube", top_bit)
    held_one = jnp.concatenate(
        [jnp.where(stay[:, None], vectors, jnp.zeros((), jnp.bfloat16)), got_rows], axis=0
    )
    tags = jnp.concatenate([jnp.where(stay, later, -1), got_tags], axis=0)
    live_one = tags >= 0
    slot_one = (jnp.arange(2) == bit_one).astype(jnp.float32)
    part_one = slot_one[:, None] * jnp.sum(held_one, axis=0, dtype=jnp.float32)[None]
    tally_one = slot_one * jnp.sum(live_one).astype(jnp.float32)
    total_one, number_one = lax.psum((part_one, tally_one), "cube")
    centre_one = total_one / number_one[:, None]
    margin_one = split_margin(held_one, live_one, centre_one, width)
    moving = live_one & (tags != bit_two)
    out_rows = compact(moving, held_one, cap_two, 0)
    out_tags = compact(moving, tags, cap_two, -1)
    in_rows, in_tags = (
        from_partner(out_rows, "cube", next_bit),
        from_partner(shortened(out_tags), "cube", next_bit).astype(out_tags.dtype),
    )
    held_two = jnp.concatenate(
        [jnp.where(moving[:, None], jnp.zeros((), jnp.bfloat16), held_one), in_rows], axis=0
    )
    live_two = jnp.concatenate([live_one & jnp.logical_not(moving), in_tags >= 0], axis=0)
    slot_two = (jnp.arange(4) == 2 * bit_one + bit_two).astype(jnp.float32)
    part_two = slot_two[:, None] * jnp.sum(held_two, axis=0, dtype=jnp.float32)[None]
    tally_two = slot_two * jnp.sum(live_two).astype(jnp.float32)
    total_two, number_two = lax.psum((part_two, tally_two), "cube")
    centre_two = total_two / number_two[:, None]
    pair = lax.dynamic_slice_in_dim(centre_two, 2 * bit_one, 2, 0)
    margin_two = split_margin(held_two, live_two, pair, width)
    centroids = jnp.concatenate([centre_one, centre_two], axis=0)
    return (held_two, margin_one, margin_two, centroids)


def solution(mesh):
    return jax.shard_map(
        local,
        mesh=mesh,
        in_specs=(P("cube", None), P(None, "cube")),
        out_specs=(P("cube", None), P("cube"), P("cube"), P()),
        check_vma=False,
    )
```

profile of v0, /device:TPU:0, one launch (start us, length us, event | category | flops | bytes accessed | tf_op | source)
XLA Modules:
  0.0 322.3 jit_solution(18157706158727844442)
XLA Ops:
  0.6 0.8 slice.61
  1.4 0.8 fusion.21
  2.2 0.3 reduce-window.16
  2.7 0.1 slice_reduce_fusion.1
  2.8 0.8 compare_select_fusion.1
  3.6 15.5 %scatter_custom_fusion = s32[2049]{0:T(1024)S(1)} fusion(s32[4096]{0:T(1024)S(1)} %bitcast.34, s32[4096]{0:T(1024)S(1)} %bitcast.30, s32[]{:T(128)} %constant.18.clone.1), kind=kCustom, calls=%fused_computation.44 | custom fusion | bytes 8200 | tf_op jit(solution)/shard_map/scatter | solution.py:23
  19.2 4.1 %collective-permute-start = (s32[2048]{0:T(1024)S(1)}, s32[2048]{0:T(1024)S(1)}, u32[]{:S(2)}, u32[]{:S(2)}) collective-permute-start(s32[2048]{0:T(1024)S(1)} %slice.80), channel_id=1, source_target_pairs={{0,16},{1,17},{2,18},{3,19},{4,20},{5,21},{6,22},{7,23},{8,24},{9,... | collective-permute-start | bytes 24584 | tf_op jit(solution)/shard_map/ppermute | solution.py:8
  23.3 20.0 %scatter_custom_fusion.1 = bf16[2049,768]{1,0:T(8,128)(2,1)S(1)} fusion(s32[4096]{0:T(1024)S(1)} %bitcast.35, bf16[4096,768]{1,0:T(8,128)(2,1)} %param.2, bf16[]{:T(256)} %constant.23.clone.1), kind=kCustom, calls=%fused_computation.10 | custom fusion | bytes 3147776 | tf_op jit(solution)/shard_map/scatter | solution.py:23
  43.3 1.9 slice.81
  45.2 2.0 copy-done
  47.2 4.1 %broadcast_select_fusion.1 = bf16[4096,768]{1,0:T(8,128)(2,1)} fusion(bf16[4096,768]{1,0:T(8,128)(2,1)S(1)} %copy-done, pred[4096]{0:T(1024)(128)(4,1)S(1)} %not.10), kind=kLoop, calls=%fused_computation.9 | loop fusion | flops 3145728 | bytes 12587008 | tf_op jit(solution)/shard_map/jit(_where)/select_n | solution.py:51
  51.4 0.6 convert_reduce_fusion.3
  52.7 0.3 reduce-window.24
  53.4 23.0 %scatter_custom_fusion.3 = s32[1025]{0:T(1024)S(1)} fusion(s32[6144]{0:T(1024)S(1)} %bitcast.32, s32[6144]{0:T(1024)S(1)} %pad_add_fusion.1, s32[]{:T(128)} %constant.18.clone.1), kind=kCustom, calls=%fused_computation.46 | custom fusion | bytes 4104 | tf_op jit(solution)/shard_map/scatter | solution.py:23
  76.4 1.6 collective-permute-start.3
  78.0 35.0 %collective-permute-done.3 = s32[1024]{0:T(1024)S(1)} collective-permute-done((s32[1024]{0:T(1024)S(1)}, s32[1024]{0:T(1024)S(1)}, u32[]{:S(2)}, u32[]{:S(2)}) %collective-permute-start.3) | collective-permute-done | bytes 4128 | tf_op jit(solution)/shard_map/ppermute | solution.py:8
  113.0 0.6 convert_reduce_fusion.2
  114.3 69.1 %collective-permute-done.1 = bf16[2048,768]{1,0:T(8,128)(2,1)} collective-permute-done((bf16[2048,768]{1,0:T(8,128)(2,1)}, bf16[2048,768]{1,0:T(8,128)(2,1)}, u32[]{:S(2)}, u32[]{:S(2)}) %collective-permute-start.1) | collective-permute-done | bytes 3145760 | tf_op jit(solution)/shard_map/ppermute | solution.py:8
  183.4 31.4 %scatter_custom_fusion.2 = bf16[1025,768]{1,0:T(8,128)(2,1)} fusion(s32[6144]{0:T(1024)S(1)} %bitcast.33, bf16[]{:T(256)} %constant.23.clone.1, bf16[2048,768]{1,0:T(8,128)(2,1)} %collective-permute-done.1, bf16[4096,768]{1,0:T(8,128)(2,1)} %broadcast_select_fusion.1), kind=kCustom, calls=%fused_computation.12 | custom fusion | flops 18874368 | bytes 11011586 | tf_op jit(solution)/shard_map/scatter | solution.py:23
  214.7 2.8 slice.84
  217.6 5.1 %convert_reduce_fusion.1 = f32[768]{0:T(1024)S(1)} fusion(bf16[2048,768]{1,0:T(8,128)(2,1)} %collective-permute-done.1, bf16[4096,768]{1,0:T(8,128)(2,1)} %broadcast_select_fusion.1), kind=kLoop, calls=%fused_computation.5 | loop fusion | flops 23592192 | bytes 9440256 | tf_op jit(solution)/shard_map/reduce_sum | solution.py:56
  222.7 7.0 %broadcast_select_fusion = bf16[6144,768]{1,0:T(8,128)(2,1)S(1)} fusion(pred[6144]{0:T(1024)(128)(4,1)S(1)} %get-tuple-element.13, bf16[2048,768]{1,0:T(8,128)(2,1)} %collective-permute-done.1, bf16[4096,768]{1,0:T(8,128)(2,1)S(1)} %bitcast.22), kind=kLoop, calls=%fused_computation.8 | loop fusion | flops 23592960 | bytes 18880512 | tf_op jit(solution)/shard_map/jit(_where)/select_n | solution.py:69
  229.8 23.4 %collective-permute-done.2 = bf16[1024,768]{1,0:T(8,128)(2,1)} collective-permute-done((bf16[1024,768]{1,0:T(8,128)(2,1)}, bf16[1024,768]{1,0:T(8,128)(2,1)}, u32[]{:S(2)}, u32[]{:S(2)}) %collective-permute-start.2) | collective-permute-done | bytes 1572896 | tf_op jit(solution)/shard_map/ppermute | solution.py:8
  253.1 11.5 %convert_reduce_fusion = (f32[768]{0:T(1024)S(1)}, bf16[7168,768]{1,0:T(8,128)(2,1)}) fusion(bf16[1024,768]{1,0:T(8,128)(2,1)} %collective-permute-done.2, bf16[6144,768]{1,0:T(8,128)(2,1)S(1)} %broadcast_select_fusion), kind=kLoop, calls=%fused_computation.4 | loop fusion | flops 33029376 | bytes 22023168 | tf_op jit(solution)/shard_map/reduce_sum | solution.py:73
  264.7 39.3 %all-reduce = (f32[2,768]{1,0:T(2,128)S(1)}, f32[2]{0:T(128)S(1)}, f32[4,768]{1,0:T(4,128)S(1)}, f32[4]{0:T(128)S(1)}) all-reduce(f32[2,768]{1,0:T(2,128)S(1)} %broadcast_multiply_fusion.1, f32[2]{0:T(128)S(1)} %compare_select_fusion.3, f32[4,768]{1,0:T(4,128)S(1)} %broadcast_multiply_fusion, ...), channel_id=1, replica_groups=mesh['cube'=32] {'cube'}, use_global_device_ids=true, to_apply=%region_8.9 | all-reduce | flops 4614 | bytes 36912 | tf_op jit(solution)/shard_map/psum | solution.py:58
  304.1 0.6 fusion.16
  306.0 5.1 %fusion.13 = f32[6144,2]{0,1:T(2,128)S(1)} fusion(f32[2,768]{1,0:T(2,128)S(1)} %broadcast_divide_fusion.1, bf16[2048,768]{1,0:T(8,128)(2,1)} %collective-permute-done.1, bf16[4096,768]{1,0:T(8,128)(2,1)} %broadcast_select_fusion.1), kind=kOutput, calls=%fused_computation.54 | convolution fusion | flops 37750272 | bytes 9492480 | tf_op jit(solution)/shard_map/dot_general | solution.py:27
  311.2 0.6 broadcast_select_fusion.3
  311.9 0.6 pad_maximum_fusion.2
  312.5 0.7 fusion.18
  314.5 7.1 %fusion.12 = f32[7168,2]{0,1:T(2,128)S(1)} fusion(bf16[7168,768]{1,0:T(8,128)(2,1)} %get-tuple-element.16, f32[4,768]{1,0:T(4,128)S(1)} %broadcast_divide_fusion, s32[]{:T(128)S(6)} %select_n.85), kind=kOutput, calls=%fused_computation.49 | convolution fusion | flops 22020096 | bytes 11070468 | tf_op jit(solution)/shard_map/dot_general | solution.py:27
  321.6 0.6 broadcast_select_fusion.2
  (35 shorter events, 1.1 us)
Async XLA Ops:
  19.2 32.1 %collective-permute-start = (s32[2048]{0:T(1024)S(1)}, s32[2048]{0:T(1024)S(1)}, u32[]{:S(2)}, u32[]{:S(2)}) collective-permute-start(s32[2048]{0:T(1024)S(1)} %slice.80), channel_id=1, source_target_pairs={{0,16},{1,17},{2,18},{3,19},{4,20},{5,21},{6,22},{7,23},{8,24},{9,... | collective-permute-start | bytes 24584 | tf_op jit(solution)/shard_map/ppermute | solution.py:8
  43.3 3.9 %copy-start = (bf16[4096,768]{1,0:T(8,128)(2,1)S(1)}, bf16[4096,768]{1,0:T(8,128)(2,1)}, u32[]{:S(2)}) copy-start(bf16[4096,768]{1,0:T(8,128)(2,1)} %param.2) | copy-start | bytes 18874372
  45.2 138.2 %collective-permute-start.1 = (bf16[2048,768]{1,0:T(8,128)(2,1)}, bf16[2048,768]{1,0:T(8,128)(2,1)}, u32[]{:S(2)}, u32[]{:S(2)}) collective-permute-start(bf16[2048,768]{1,0:T(8,128)(2,1)} %slice.81), channel_id=1, source_target_pairs={{0,16},{1,17},{2,18},{3,19},{4,20},{5,21},{6,22},{7,23},{8,24},{9,... | collective-permute-start | bytes 9437192 | tf_op jit(solution)/shard_map/ppermute | solution.py:8
  76.4 36.6 %collective-permute-start.3 = (s32[1024]{0:T(1024)S(1)}, s32[1024]{0:T(1024)S(1)}, u32[]{:S(2)}, u32[]{:S(2)}) collective-permute-start(s32[1024]{0:T(1024)S(1)} %slice.89), channel_id=1, source_target_pairs={{0,8},{1,9},{2,10},{3,11},{4,12},{5,13},{6,14},{7,15},{8,0},{9,1},... | collective-permute-start | bytes 12296 | tf_op jit(solution)/shard_map/ppermute | solution.py:8
  114.3 108.4 %slice-start = ((s8[6291456]{0:T(1024)(128)(4,1)}), s8[2097152]{0:T(1024)(128)(4,1)S(1)}, s32[]{:S(2)}) async-start(s8[6291456]{0:T(1024)(128)(4,1)} %bitcast.21), calls=%async_computation | async-start | bytes 4194304
  214.7 8.0 %slice-start.1 = ((s8[6291456]{0:T(1024)(128)(4,1)}), s8[4194304]{0:T(1024)(128)(4,1)S(1)}, s32[]{:S(2)}) async-start(s8[6291456]{0:T(1024)(128)(4,1)} %bitcast.21), calls=%async_computation.1 | async-start | bytes 8388608
  217.6 35.6 %collective-permute-start.2 = (bf16[1024,768]{1,0:T(8,128)(2,1)}, bf16[1024,768]{1,0:T(8,128)(2,1)}, u32[]{:S(2)}, u32[]{:S(2)}) collective-permute-start(bf16[1024,768]{1,0:T(8,128)(2,1)} %slice.84), channel_id=1, source_target_pairs={{0,8},{1,9},{2,10},{3,11},{4,12},{5,13},{6,14},{7,15},{8,0},{9,1},... | collective-permute-start | bytes 4718600 | tf_op jit(solution)/shard_map/ppermute | solution.py:8
where the time goes:
time: 323 us; the launch traced here: 322 us
  waiting for transfers between devices  127 us (39%)
  other arithmetic  66.5 us (21%)
  local copies, waits for them, and re-layouts  66.4 us (21%)
  blocking collectives  39.3 us (12%)
  matrix products  12.2 us (4%)
  starting transfers between devices  5.76 us (2%)
  between operations  4.76 us (1%)
    ppermute x4, waiting for transfers between devices, from_partner(): lax.ppermute(shard, axis, [(i, i ^ 1 << stride) for i in range(lax.axis_s...  127 us
    scatter x3, local copies, waits for them, and re-layouts, compact(): return base.at[index].set(rows)[:cap]  58.5 us
    psum x1, blocking collectives, local(): total_one, number_one = lax.psum((part_one, tally_one), 'cube')  39.3 us
    scatter x1, other arithmetic, compact(): return base.at[index].set(rows)[:cap]  31.4 us
    dot_general x2, matrix products, split_margin(): jnp.dot(held_rows, pair.astype(jnp.bfloat16).T, preferred_element_type=jn...  12.2 us
    reduce_sum x1, other arithmetic, local(): jnp.sum(held_two, axis=0, dtype=jnp.float32)[None]  11.5 us
    select_n x1, other arithmetic, local(): jnp.where(moving[:, None], jnp.zeros((), jnp.bfloat16), held_one)  7.02 us
  transfers between devices with their start and end apart: 4, of which 3 were waited for; matrix products, arithmetic and copies ran while one was open for 20% of the time, Pallas kernels for 0%

commit v1 on v0

v1 whole, which is shorter than its diff:
```python
import functools
import jax
import jax.numpy as jnp
from jax import lax
from jax.experimental import pallas as pl
from jax.experimental.pallas import tpu as pltpu
from jax.sharding import PartitionSpec as P

BF = jnp.bfloat16
F32 = jnp.float32
I32 = jnp.int32
BLK = 256
PARTS = 4
VMEM_BYTES = 48 * 1024 * 1024


def swap(x, bits):
    return lax.ppermute(x, "cube", [(i, i ^ bits) for i in range(lax.axis_size("cube"))])


def dot(a, b):
    return lax.dot_general(a, b, (((1,), (0,)), ((), ())), preferred_element_type=F32)


def dot_t(a, b):
    return lax.dot_general(a, b, (((1,), (1,)), ((), ())), preferred_element_type=F32)


def iota(shape, dim):
    return lax.broadcasted_iota(I32, shape, dim)


def as_bf(mask):
    return jnp.where(mask, jnp.float32(1), jnp.float32(0)).astype(BF)


def pack(sums, counts, width):
    high = sums.astype(BF).astype(F32)
    middle = (sums - high).astype(BF).astype(F32)
    low = sums - high - middle
    spare = width - 128 * len(counts)
    counts = jnp.concatenate(counts + ([jnp.zeros((1, spare), I32)] if spare else []), axis=1)
    upper, lower = (counts >> 8).astype(F32), (counts & 255).astype(F32)
    return jnp.concatenate([high, middle, low, upper, lower, jnp.zeros((2, width), F32)], axis=0).astype(BF)


def unpack(extra):
    extra = extra.astype(F32)
    sums = extra[0:4] + extra[4:8] + extra[8:12]
    return sums, extra[12:13] * 256.0 + extra[13:14]


def count_at(extra, k):
    extra = extra[12:14, 128 * k : 128 * k + 1].astype(F32)
    return (extra[0:1] * 256.0 + extra[1:2]).astype(I32)


def spec(memory):
    return pl.BlockSpec(memory_space=memory)


def params():
    return pltpu.CompilerParams(vmem_limit_bytes=VMEM_BYTES)


def sort_kernel(here, labels, x_hbm, *refs):
    outs, (pos_ref, off_ref, x, buf, tail, sem_in, sem_out) = refs[:PARTS], refs[PARTS:]
    rows = labels.shape[1]
    blocks = rows // BLK
    cap = rows // 2
    step = rows // PARTS
    loads = [
        pltpu.make_async_copy(x_hbm.at[pl.ds(k * step, step)], x.at[pl.ds(k * step, step)], sem_in.at[k])
        for k in range(PARTS)
    ]
    for load in loads:
        load.start()
    buf[...] = jnp.zeros_like(buf)
    leave = labels[0:1, :] != here[0]
    miss = labels[1:2, :] != here[1]
    code = jnp.where(leave, jnp.where(miss, 0, 1), jnp.where(miss, 2, 3))
    code = jnp.concatenate(
        [jnp.broadcast_to(code[:, b * BLK : (b + 1) * BLK], (8, BLK)) for b in range(blocks)], axis=0
    )
    tall = 8 * blocks
    kind = iota((tall, BLK), 0) & 7
    mask = (code == kind) | ((kind == 4) & (code <= 1))
    maskb = as_bf(mask)
    upper = as_bf(iota((BLK, BLK), 0) <= iota((BLK, BLK), 1))
    before = dot(maskb, upper)
    total = dot(maskb, jnp.ones((BLK, BLK), BF)).astype(BF)
    r, c = iota((tall, tall), 0), iota((tall, tall), 1)
    same = ((r ^ c) & 7) == 0
    earlier = as_bf((same & (c < r)) | (((r & 7) == 1) & ((c & 7) == 0)))
    off = dot(earlier, total)
    pos_ref[...] = jnp.where(mask, (before + off).astype(I32) - 1, -1)
    off_ref[...] = off[:, :128].astype(I32)
    r8, c8 = iota((8, tall), 0), iota((8, tall), 1)
    every = dot(as_bf(r8 == (c8 & 7)), total)[:, :128].astype(I32)
    group = 2 * labels[0:1, :] + labels[1:2, :]
    wide = BLK + 16
    slot = iota((wide, BLK), 0)
    sums = jnp.zeros((4, x.shape[1]), F32)
    for b in range(blocks):
        if b % (step // BLK) == 0:
            loads[b // (step // BLK)].wait()
        hot = []
        bases = []
        for kind in (0, 1):
            base = off_ref[8 * b + kind : 8 * b + kind + 1, 0:1]
            base = jnp.minimum((base[0, 0] // 16) * 16, cap)
            place = pos_ref[8 * b + kind : 8 * b + kind + 1, :]
            hot.append(as_bf(slot == place - base))
            bases.append(pl.multiple_of(base, 16))
        hot.append(as_bf((iota((16, BLK), 0) & 3) == group[:, b * BLK : (b + 1) * BLK]))
        got = dot(jnp.concatenate(hot, axis=0), x[b * BLK : (b + 1) * BLK, :])
        for kind in (0, 1):
            buf[pl.ds(bases[kind], wide), :] += got[kind * wide : (kind + 1) * wide].astype(BF)
        sums += got[2 * wide : 2 * wide + 4]
    one, two = here[0], here[1]
    kinds = [every[k : k + 1] for k in range(4)]
    counts = []
    for g in range(4):
        away, miss = jnp.int32(g >> 1) != one, jnp.int32(g & 1) != two
        counts.append(jnp.where(away, jnp.where(miss, kinds[0], kinds[1]), jnp.where(miss, kinds[2], kinds[3])))
    tail[...] = pack(sums, counts + [kinds[0], kinds[2]], x.shape[1])
    part = cap // PARTS
    stores = [
        pltpu.make_async_copy(buf.at[pl.ds(k * part, part)], outs[k].at[pl.ds(0, part)], sem_out.at[k])
        for k in range(PARTS)
    ]
    stores.append(pltpu.make_async_copy(tail, outs[0].at[pl.ds(part, 16)], sem_out.at[PARTS]))
    for store in stores:
        store.start()
    for store in stores:
        store.wait()


def sort_call(here, labels, vectors):
    rows, width = vectors.shape
    tall = 8 * rows // BLK
    part = rows // 2 // PARTS
    return pl.pallas_call(
        sort_kernel,
        out_shape=[jax.ShapeDtypeStruct((part + (0 if k else 16), width), BF) for k in range(PARTS)]
        + [
            jax.ShapeDtypeStruct((tall, BLK), I32),
            jax.ShapeDtypeStruct((tall, 128), I32),
        ],
        in_specs=[spec(pltpu.SMEM), spec(pltpu.VMEM), spec(pl.ANY)],
        out_specs=[spec(pl.ANY)] * PARTS + [spec(pltpu.VMEM)] * 2,
        scratch_shapes=[
            pltpu.VMEM((rows, width), BF),
            pltpu.VMEM((rows // 2 + BLK + 16, width), BF),
            pltpu.VMEM((16, width), BF),
            pltpu.SemaphoreType.DMA((PARTS,)),
            pltpu.SemaphoreType.DMA((PARTS + 1,)),
        ],
        compiler_params=params(),
        cost_estimate=pl.CostEstimate(flops=8 * 10**9, bytes_accessed=10 * 10**6, transcendentals=0),
        name="sort_leavers",
    )(here, labels, vectors)


def stay_kernel(off, pos, extra, x_ref, held, second, meta, buf, ranks):
    b = pl.program_id(0)

    @pl.when(b == 0)
    def _():
        buf[...] = jnp.zeros_like(buf)
        ranks[...] = jnp.zeros_like(ranks)

    x = x_ref[...]
    half = second.shape[0] - 16
    cap = 4 * half
    stays = pos[3:4, :] >= 0
    diag = as_bf((iota((BLK, BLK), 0) == iota((BLK, BLK), 1)) & stays)
    base = jnp.minimum((off[8 * b + 2, 0] // 16) * 16, half)
    wide = BLK + 16
    hot = as_bf(iota((wide, BLK), 0) == pos[2:3, :] - base)
    got = dot(jnp.concatenate([diag, hot], axis=0), x)
    held[...] = got[:BLK].astype(BF)
    buf[pl.ds(pl.multiple_of(base, 16), wide), :] += got[BLK:].astype(BF)
    rank = pos[4:5, :]
    line = iota((16, BLK), 0)
    value = jnp.where(line == 0, rank >> 8, jnp.where(line == 1, rank & 255, 1))
    value = jnp.where(rank >= 0, value, 0).astype(F32).astype(BF)
    for kind in (0, 1):
        base = pl.multiple_of(jnp.minimum((off[8 * b + kind, 0] // 128) * 128, cap), 128)
        hot = as_bf(iota((BLK + 128, BLK), 0) == pos[kind : kind + 1, :] - base)
        ranks[:, pl.ds(base, BLK + 128)] += dot_t(value, hot)[:8]

    @pl.when(b == pl.num_programs(0) - 1)
    def _():
        second[0:half, :] = buf[0:half, :]
        second[half:, :] = extra[...]
        seen = ranks[2:3, :cap] > 0.5
        rank = (ranks[0:1, :cap] * 256.0 + ranks[1:2, :cap]).astype(I32)
        goal = jnp.where(seen, rank, 1 << 20)
        line = cap // 8
        for k in range(8):
            meta[k : k + 1, :] = goal[:, k * line : (k + 1) * line]


def stay_call(off, pos, first, vectors):
    rows, width = vectors.shape
    cap = rows // 2
    half = rows // 8
    return pl.pallas_call(
        stay_kernel,
        grid=(rows // BLK,),
        out_shape=[
            jax.ShapeDtypeStruct((rows + cap + cap // 2, width), BF),
            jax.ShapeDtypeStruct((half + 16, width), BF),
            jax.ShapeDtypeStruct((8, cap // 8), I32),
        ],
        in_specs=[
            spec(pltpu.SMEM),
            pl.BlockSpec((8, BLK), lambda b: (b, 0)),
            pl.BlockSpec((16, width), lambda b: (half // 16, 0)),
            pl.BlockSpec((BLK, width), lambda b: (b, 0)),
        ],
        out_specs=[
            pl.BlockSpec((BLK, width), lambda b: (b, 0)),
            pl.BlockSpec((half + 16, width), lambda b: (0, 0)),
            pl.BlockSpec((8, cap // 8), lambda b: (0, 0)),
        ],
        scratch_shapes=[pltpu.VMEM((half + BLK + 16, width), BF), pltpu.VMEM((8, cap + BLK + 128), F32)],
        compiler_params=params(),
        cost_estimate=pl.CostEstimate(flops=6 * 10**9, bytes_accessed=14 * 10**6, transcendentals=0),
        name="own_slots",
    )(off, pos, first, vectors)


def margins(score, shift, first, width):
    return (score[first + 1 : first + 2] - score[first : first + 1] - shift) / width


def put_lines(ref, start, values):
    for k in range(values.shape[1] // 128):
        ref[start + k : start + k + 1, :] = values[:, 128 * k : 128 * (k + 1)]


def centre_kernel(here, total, labels, x_ref, cents, centres, shifts, one, two):
    width = x_ref.shape[1]

    @pl.when(pl.program_id(0) == 0)
    def _():
        sums, counts = total[0:4, :], total[4:8, :]
        low = (sums[0:1] + sums[1:2]) / (counts[0:1] + counts[1:2])
        high = (sums[2:3] + sums[3:4]) / (counts[2:3] + counts[3:4])
        groups = sums / counts
        cents[0:1, :] = low
        cents[1:2, :] = high
        cents[2:6, :] = groups
        top = here[0] == 1
        left = jnp.where(top, groups[2:3], groups[0:1])
        right = jnp.where(top, groups[3:4], groups[1:2])
        centres[...] = jnp.concatenate([low, high, left, right, jnp.zeros((12, width), F32)], axis=0).astype(BF)
        for k, (a, b) in enumerate(((low, high), (left, right))):
            shift = 0.5 * (jnp.sum(b * b, axis=1, keepdims=True) - jnp.sum(a * a, axis=1, keepdims=True))
            shifts[k : k + 1, :] = jnp.broadcast_to(shift, (1, 128))

    score = dot_t(centres[...], x_ref[...])
    stay = labels[0:1, :] == here[0]
    keep = stay & (labels[1:2, :] == here[1])
    put_lines(one, 0, jnp.where(stay, margins(score, shifts[0:1, 0:1], 0, width), 0.0))
    put_lines(two, 0, jnp.where(keep, margins(score, shifts[1:2, 0:1], 2, width), 0.0))


def centre_call(here, total, labels, vectors):
    rows, width = vectors.shape
    cap = rows // 2
    return pl.pallas_call(
        centre_kernel,
        grid=(rows // 1024,),
        out_shape=[
            jax.ShapeDtypeStruct((6, width), F32),
            jax.ShapeDtypeStruct((16, width), BF),
            jax.ShapeDtypeStruct((8, 128), F32),
            jax.ShapeDtypeStruct(((rows + cap) // 128, 128), F32),
            jax.ShapeDtypeStruct(((rows + cap + cap // 2) // 128, 128), F32),
        ],
        in_specs=[
            spec(pltpu.SMEM),
            pl.BlockSpec((8, width), lambda b: (0, 0)),
            pl.BlockSpec((2, 1024), lambda b: (0, b)),
            pl.BlockSpec((1024, width), lambda b: (b, 0)),
        ],
        out_specs=[
            pl.BlockSpec((6, width), lambda b: (0, 0)),
            pl.BlockSpec((16, width), lambda b: (0, 0)),
            pl.BlockSpec((8, 128), lambda b: (0, 0)),
            pl.BlockSpec((8, 128), lambda b: (b, 0)),
            pl.BlockSpec((8, 128), lambda b: (b, 0)),
        ],
        compiler_params=params(),
        cost_estimate=pl.CostEstimate(flops=2 * 10**9, bytes_accessed=7 * 10**6, transcendentals=0),
        name="own_margins",
    )(here, total, labels, vectors)


def second_kernel(centres, shifts, second, relay, first, meta, held_in, two_in, held, two, again, start, goals):
    del held_in, two_in
    half = second.shape[0] - 16
    slots = held.shape[0]
    cap = 2 * slots
    have = count_at(second[half:, :], 5)
    more = count_at(relay[half:, :], 4)
    both = count_at(first[half:, :], 4)
    lane = iota((1, half), 1)
    goal = jnp.where(lane < more, lane + have, -1)
    moved = dot(as_bf(iota((slots, half), 0) == goal), relay[0:half, :]).astype(BF)
    held[0:half, :] = moved[0:half] + second[0:half, :]
    held[half:, :] = moved[half:]
    score = dot_t(centres[...], held[...])
    width = held.shape[1]
    live = iota((1, slots), 1) < have + more
    put_lines(two, 0, jnp.where(live, margins(score, shifts[1:2, 0:1], 2, width), 0.0))

    score = dot_t(centres[...], first[0:half, :])
    value = jnp.where(lane < both, margins(score, shifts[0:1, 0:1], 0, width), 0.0)
    high = value.astype(BF).astype(F32)
    middle = (value - high).astype(BF).astype(F32)
    low = value - high - middle
    value = jnp.concatenate([high, middle, low, jnp.zeros((13, half), F32)], axis=0).astype(BF)
    place = jnp.concatenate([meta[k : k + 1, :] for k in range(8)], axis=1)
    goal = jnp.where(lane < both, place[:, :half], -1)
    for k in range(cap // BLK):
        hot = as_bf(iota((BLK, half), 0) + k * BLK == goal)
        got = dot_t(value, hot)
        put_lines(again, k * BLK // 128, got[0:1] + got[1:2] + got[2:3])
    lane = iota((8, cap), 1)
    earlier = (lane < both) | (place < BLK * iota((8, cap), 0))
    begin = jnp.sum(jnp.where(earlier, 1.0, 0.0), axis=1, keepdims=True).astype(I32)
    begin = jnp.minimum((begin >> 7) << 7, cap - BLK - 128)
    start[...] = jnp.broadcast_to(begin, start.shape)
    goals[...] = jnp.broadcast_to(jnp.where(iota((1, cap), 1) < both, -1, place), goals.shape)


def second_call(centres, shifts, second, relay, first, meta, held, two):
    half, width = second.shape
    half -= 16
    cap = 4 * half
    slots = cap // 2
    return pl.pallas_call(
        second_kernel,
        grid=(1,),
        out_shape=[
            jax.ShapeDtypeStruct(held.shape, BF),
            jax.ShapeDtypeStruct(two.shape, F32),
            jax.ShapeDtypeStruct((cap // 128, 128), F32),
            jax.ShapeDtypeStruct((8, 128), I32),
            jax.ShapeDtypeStruct((8, cap), I32),
        ],
        in_specs=[spec(pltpu.VMEM)] * 6 + [spec(pl.ANY)] * 2,
        out_specs=[
            pl.BlockSpec((slots, width), lambda b: (held.shape[0] // slots - 1, 0)),
            pl.BlockSpec((slots // 128, 128), lambda b: (held.shape[0] // slots - 1, 0)),
            pl.BlockSpec((cap // 128, 128), lambda b: (0, 0)),
            pl.BlockSpec((8, 128), lambda b: (0, 0)),
            pl.BlockSpec((8, cap), lambda b: (0, 0)),
        ],
        input_output_aliases={6: 0, 7: 1},
        compiler_params=params(),
        cost_estimate=pl.CostEstimate(flops=3 * 10**9, bytes_accessed=6 * 10**6, transcendentals=0),
        name="second_slots",
    )(centres, shifts, second, relay, first, meta, held, two)


def column_kernel(own, a, b, c, out):
    sums, counts = unpack(own[...])
    for other in (a, b, c):
        s, n = unpack(other[...])
        sums, counts = sums + s, counts + n
    out[0:4, :] = sums
    width = out.shape[1]
    for g in range(4):
        out[4 + g : 5 + g, :] = jnp.broadcast_to(counts[:, 128 * g : 128 * g + 1], (1, width))


def column_call(*pieces):
    rows, width = pieces[0].shape
    return pl.pallas_call(
        column_kernel,
        grid=(1,),
        out_shape=jax.ShapeDtypeStruct((8, width), F32),
        in_specs=[pl.BlockSpec((16, width), lambda b: (rows // 16 - 1, 0))] * 4,
        out_specs=pl.BlockSpec((8, width), lambda b: (0, 0)),
        compiler_params=params(),
        name="column_sums",
    )(*pieces)


def first_kernel(start, centres, shifts, goals, again, *refs):
    pieces, (held_in, one_in, two_in, held, one, two, x, sem) = refs[:PARTS], refs[PARTS:]
    del held_in, one_in, two_in
    k = pl.program_id(0)
    part, width = pieces[1].shape

    @pl.when(k == 0)
    def _():
        loads = [
            pltpu.make_async_copy(pieces[i].at[pl.ds(0, part)], x.at[pl.ds(i * part, part)], sem.at[i])
            for i in range(PARTS)
        ]
        for load in loads:
            load.start()
        for load in loads:
            load.wait()

    span = BLK + 128
    begin = pl.multiple_of(start[k, 0], 128)
    goal = goals[0:1, pl.ds(begin, span)] - k * BLK
    hot = as_bf(iota((BLK, span), 0) == goal)
    rows = dot(hot, x[pl.ds(begin, span), :]).astype(BF)
    held[...] = rows
    score = dot_t(centres[...], rows)
    live = dot_t(jnp.ones((16, span), BF), hot)[0:1] > 0.5
    m_one = margins(score, shifts[0:1, 0:1], 0, width)
    m_two = margins(score, shifts[1:2, 0:1], 2, width)
    for i in range(BLK // 128):
        line = k * (BLK // 128) + i
        part_live = live[:, 128 * i : 128 * (i + 1)]
        one[pl.ds(line, 1), :] = jnp.where(part_live, m_one[:, 128 * i : 128 * (i + 1)], again[pl.ds(line, 1), :])
        two[pl.ds(line, 1), :] = jnp.where(part_live, m_two[:, 128 * i : 128 * (i + 1)], 0.0)


def first_call(start, centres, shifts, goals, again, pieces, held, one, two):
    width = held.shape[1]
    cap = goals.shape[1]
    base = 2 * cap // BLK
    lines = cap // 128
    return pl.pallas_call(
        first_kernel,
        grid=(cap // BLK,),
        out_shape=[
            jax.ShapeDtypeStruct(held.shape, BF),
            jax.ShapeDtypeStruct(one.shape, F32),
            jax.ShapeDtypeStruct(two.shape, F32),
        ],
        in_specs=[spec(pltpu.SMEM)] + [spec(pltpu.VMEM)] * 4 + [spec(pl.ANY)] * (PARTS + 3),
        out_specs=[
            pl.BlockSpec((BLK, width), lambda k: (base + k, 0)),
            pl.BlockSpec((lines, 128), lambda k: (2, 0)),
            pl.BlockSpec((lines, 128), lambda k: (2, 0)),
        ],
        scratch_shapes=[pltpu.VMEM((cap, width), BF), pltpu.SemaphoreType.DMA((PARTS,))],
        input_output_aliases={5 + PARTS: 0, 6 + PARTS: 1, 7 + PARTS: 2},
        compiler_params=params(),
        cost_estimate=pl.CostEstimate(flops=3 * 10**9, bytes_accessed=7 * 10**6, transcendentals=0),
        name="first_slots",
    )(start, centres, shifts, goals, again, *pieces, held, one, two)


def local(vectors, child_labels):
    ways = lax.axis_size("cube")
    top = ways // 2
    nxt = ways // 4
    me = lax.axis_index("cube")
    here = jnp.stack([(me // top) & 1, (me // nxt) & 1]).astype(I32)
    *pieces, pos, off = sort_call(here, child_labels, vectors)
    got = []
    for k, piece in enumerate(pieces):
        if k >= 2:
            piece, got[k - 2] = lax.optimization_barrier((piece, got[k - 2]))
        got.append(swap(piece, top))
    held, second, meta = stay_call(off, pos, pieces[0], vectors)
    second_in = swap(second, nxt)
    meta_in = swap(meta, top)
    relay = swap(got[0], nxt)
    total = column_call(pieces[0], second_in, got[0], relay)
    bit = 1
    while bit < nxt:
        total = total + swap(total, bit)
        bit *= 2
    cents, centres, shifts, one, two = centre_call(here, total, child_labels, vectors)
    held, two, again, start, goals = second_call(centres, shifts, second_in, relay, got[0], meta_in, held, two)
    held, one, two = first_call(start, centres, shifts, goals, again, got, held, one, two)
    return held, one.reshape(-1), two.reshape(-1), cents


def solution(mesh):
    return jax.shard_map(
        local,
        mesh=mesh,
        in_specs=(P("cube", None), P(None, "cube")),
        out_specs=(P("cube", None), P("cube"), P("cube"), P()),
        check_vma=False,
    )
```

time: 323 us -> 163 us (0.50)
  other arithmetic: 66.5 us -> 0.09 us
  local copies, waits for them, and re-layouts: 66.4 us -> 0.76 us
  blocking collectives: 39.3 us -> 0 us
  Pallas kernels: 0 us -> 38 us
  waiting for transfers between devices: 127 us -> 111 us
  matrix products: 12.2 us -> 0 us
  starting transfers between devices: 5.76 us -> 12.5 us
  between operations: 4.76 us -> 0.69 us
    scatter x3 -> x0, local copies, waits for them, and re-layouts: 58.5 us -> none  [compact(): return base.at[index].set(rows)[:cap]]
    psum x1 -> x0, blocking collectives: 39.3 us -> none  [local(): total_one, number_one = lax.psum((part_one, tally_one), 'cube')]
    pallas_call x0 -> x6, Pallas kernels: none -> 38 us  [the longest x1 15 us: stay_call(): pl.pallas_call(stay_kernel, grid=(rows // BLK,), out_shape=[jax.ShapeDtyp...]
    scatter x1 -> x0, other arithmetic: 31.4 us -> none  [compact(): return base.at[index].set(rows)[:cap]]
    reduce_sum x6 -> x0, other arithmetic: 19.2 us -> none  [the longest x1 11.5 us: local(): jnp.sum(held_two, axis=0, dtype=jnp.float32)[None]]
    ppermute x4 -> x10, waiting for transfers between devices: 127 us -> 111 us  [swap(): lax.ppermute(x, 'cube', [(i, i ^ bits) for i in range(lax.axis_size('cube...]
    select_n x7 -> x0, other arithmetic: 13.2 us -> none  [the longest x1 7.02 us: local(): jnp.where(moving[:, None], jnp.zeros((), jnp.bfloat16), held_one)]
    dot_general x2 -> x0, matrix products: 12.2 us -> none  [split_margin(): jnp.dot(held_rows, pair.astype(jnp.bfloat16).T, preferred_element_type=jn...]
  transfers between devices with their start and end apart: 4 -> 10, of which waited for: 3 -> 7; matrix products, arithmetic and copies ran while one was open for 20% -> 0% of each run, Pallas kernels for 0% -> 14%
where the time goes in v1:
time: 163 us
  waiting for transfers between devices  111 us (68%)
  Pallas kernels  38 us (23%)
  starting transfers between devices  12.5 us (8%)
    ppermute x10, waiting for transfers between devices, swap(): lax.ppermute(x, 'cube', [(i, i ^ bits) for i in range(lax.axis_size('cube...  111 us
    pallas_call x1, Pallas kernels, stay_call(): pl.pallas_call(stay_kernel, grid=(rows // BLK,), out_shape=[jax.ShapeDtyp...  15 us
    ppermute x10, starting transfers between devices, swap(): lax.ppermute(x, 'cube', [(i, i ^ bits) for i in range(lax.axis_size('cube...  12.5 us
    pallas_call x1, Pallas kernels, sort_call(): pl.pallas_call(sort_kernel, out_shape=[jax.ShapeDtypeStruct((part + (0 if...  8.84 us
    pallas_call x1, Pallas kernels, first_call(): pl.pallas_call(first_kernel, grid=(cap // BLK,), out_shape=[jax.ShapeDtyp...  6.13 us
    pallas_call x1, Pallas kernels, centre_call(): pl.pallas_call(centre_kernel, grid=(rows // 1024,), out_shape=[jax.ShapeD...  5.42 us
  transfers between devices with their start and end apart: 10, of which 7 were waited for; matrix products, arithmetic and copies ran while one was open for 0% of the time, Pallas kernels for 14%

profile of v1, /device:TPU:0, one launch (start us, length us, event | category | flops | bytes accessed | tf_op | source)
XLA Modules:
  0.0 162.7 jit_solution(13600717444735971368)
XLA Ops:
  0.7 0.1 pad_add_fusion.here
  0.7 0.0 copy-start
  0.7 0.8 copy-done
  1.5 8.8 %sort_leavers.1 = (bf16[528,768]{1,0:T(8,128)(2,1)S(1)}, bf16[512,768]{1,0:T(8,128)(2,1)S(1)}, bf16[512,768]{1,0:T(8,128)(2,1)S(1)}, bf16[512,768]{1,0:T(8,128)(...) custom-call(s32[2]{0:T(128)S(1)} %pad_add_fusion.here, s32[2,4096]{1,0:T(2,128)S(1)} %copy-done, ...), custom_call_target="tpu_custom_call" | custom-call | flops 8000000000 | bytes 10000000 | tf_op jit(solution)/shard_map/sort_leavers/pallas_call | solution.py:143
  10.3 4.0 %collective-permute-start.1 = (bf16[528,768]{1,0:T(8,128)(2,1)S(1)}, bf16[528,768]{1,0:T(8,128)(2,1)S(1)}, u32[]{:S(2)}, u32[]{:S(2)}) collective-permute-start(bf16[528,768]{1,0:T(8,128)(2,1)S(1)} %get-tuple-element.30.extra.own), channel_id=1, source_target_pairs={{0,16},{1,17},{2,18},{3,19},{4,20},{5,21},{6,22},{7,23},{8,24},{9,... | collective-permute-start | bytes 2433032 | tf_op jit(solution)/shard_map/ppermute | solution.py:18
  14.4 0.1 collective-permute-start.7
  14.5 15.0 %own_slots.1 = (bf16[7168,768]{1,0:T(8,128)(2,1)}, bf16[528,768]{1,0:T(8,128)(2,1)S(1)}, s32[8,256]{1,0:T(8,128)S(1)}) custom-call(s32[128,128]{1,0:T(8,128)S(1)} %get-tuple-element.31.off, s32[128,256]{1,0:T(8,128)S(1)} %get-tuple-element.32.pos, bf16[528,768]{1,0:T(8,128)(2,1)S(1)} %get-tuple-element.30.extra.own, bf16[4096,768]{1,0:T(8,128)(2,1)} %x_ref.3), custom_call_target="tpu_custom_call" | custom-call | flops 6000000000 | bytes 14000000 | tf_op jit(solution)/shard_map/own_slots/pallas_call | solution.py:209
  29.5 1.9 %collective-permute-start = (bf16[528,768]{1,0:T(8,128)(2,1)S(1)}, bf16[528,768]{1,0:T(8,128)(2,1)S(1)}, u32[]{:S(2)}, u32[]{:S(2)}) collective-permute-start(bf16[528,768]{1,0:T(8,128)(2,1)S(1)} %get-tuple-element.33), channel_id=1, source_target_pairs={{0,8},{1,9},{2,10},{3,11},{4,12},{5,13},{6,14},{7,15},{8,0},{9,1},... | collective-permute-start | bytes 2433032 | tf_op jit(solution)/shard_map/ppermute | solution.py:18
  31.3 36.2 %collective-permute-done.1.b.first.refs_0_ = bf16[528,768]{1,0:T(8,128)(2,1)S(1)} collective-permute-done((bf16[528,768]{1,0:T(8,128)(2,1)S(1)}, bf16[528,768]{1,0:T(8,128)(2,1)S(1)}, u32[]{:S(2)}, u32[]{:S(2)}) %collective-permute-start.1) | collective-permute-done | bytes 811040 | tf_op jit(solution)/shard_map/ppermute | solution.py:18
  67.5 0.0 collective-permute-start.2
  67.5 16.1 %collective-permute-done.7.refs_1_ = bf16[512,768]{1,0:T(8,128)(2,1)S(1)} collective-permute-done((bf16[512,768]{1,0:T(8,128)(2,1)S(1)}, bf16[512,768]{1,0:T(8,128)(2,1)S(1)}, u32[]{:S(2)}, u32[]{:S(2)}) %collective-permute-start.7) | collective-permute-done | bytes 786464 | tf_op jit(solution)/shard_map/ppermute | solution.py:18
  83.6 0.0 collective-permute-start.9
  83.6 2.9 %collective-permute-start.8 = (bf16[512,768]{1,0:T(8,128)(2,1)S(1)}, bf16[512,768]{1,0:T(8,128)(2,1)S(1)}, u32[]{:S(2)}, u32[]{:S(2)}) collective-permute-start(bf16[512,768]{1,0:T(8,128)(2,1)S(1)} %get-tuple-element.47), channel_id=1, source_target_pairs={{0,16},{1,17},{2,18},{3,19},{4,20},{5,21},{6,22},{7,23},{8,24},{9,... | collective-permute-start | bytes 2359304 | tf_op jit(solution)/shard_map/ppermute | solution.py:18
  86.5 0.0 collective-permute-done.a.second
  86.5 16.6 %collective-permute-done.2.c.relay = bf16[528,768]{1,0:T(8,128)(2,1)S(1)} collective-permute-done((bf16[528,768]{1,0:T(8,128)(2,1)S(1)}, bf16[528,768]{1,0:T(8,128)(2,1)S(1)}, u32[]{:S(2)}, u32[]{:S(2)}) %collective-permute-start.2) | collective-permute-done | bytes 811040 | tf_op jit(solution)/shard_map/ppermute | solution.py:18
  103.1 0.1 column_sums.1
  103.2 0.0 collective-permute-start.3
  103.2 1.2 collective-permute-done.3
  104.4 1.8 %collective-permute-start.4 = (f32[8,768]{1,0:T(8,128)S(1)}, f32[8,768]{1,0:T(8,128)S(1)}, u32[]{:S(2)}, u32[]{:S(2)}) collective-permute-start(f32[8,768]{1,0:T(8,128)S(1)} %add.11), channel_id=1, source_target_pairs={{0,2},{1,3},{2,0},{3,1},{4,6},{5,7},{6,4},{7,5},{8,10},{9,11},{10,... | collective-permute-start | bytes 73736 | tf_op jit(solution)/shard_map/ppermute | solution.py:18
  106.2 2.0 %collective-permute-done.4 = f32[8,768]{1,0:T(8,128)S(1)} collective-permute-done((f32[8,768]{1,0:T(8,128)S(1)}, f32[8,768]{1,0:T(8,128)S(1)}, u32[]{:S(2)}, u32[]{:S(2)}) %collective-permute-start.4) | collective-permute-done | bytes 24608 | tf_op jit(solution)/shard_map/ppermute | solution.py:18
  108.2 1.8 %collective-permute-start.5 = (f32[8,768]{1,0:T(8,128)S(1)}, f32[8,768]{1,0:T(8,128)S(1)}, u32[]{:S(2)}, u32[]{:S(2)}) collective-permute-start(f32[8,768]{1,0:T(8,128)S(1)} %add.12), channel_id=1, source_target_pairs={{0,4},{1,5},{2,6},{3,7},{4,0},{5,1},{6,2},{7,3},{8,12},{9,13},{10,... | collective-permute-start | bytes 73736 | tf_op jit(solution)/shard_map/ppermute | solution.py:18
  110.0 0.0 collective-permute-start.6
  110.0 2.1 %collective-permute-done.5 = f32[8,768]{1,0:T(8,128)S(1)} collective-permute-done((f32[8,768]{1,0:T(8,128)S(1)}, f32[8,768]{1,0:T(8,128)S(1)}, u32[]{:S(2)}, u32[]{:S(2)}) %collective-permute-start.5) | collective-permute-done | bytes 24608 | tf_op jit(solution)/shard_map/ppermute | solution.py:18
  112.1 5.4 %own_margins.1 = (f32[6,768]{1,0:T(8,128)}, bf16[16,768]{1,0:T(8,128)(2,1)S(1)}, f32[8,128]{1,0:T(8,128)S(1)}, f32[48,128]{1,0:T(8,128)}, f32[56,128]{1,0:T(8,128)}) custom-call(s32[2]{0:T(128)S(1)} %pad_add_fusion.here, f32[8,768]{1,0:T(8,128)S(1)} %add.13.total, s32[2,4096]{1,0:T(2,128)S(1)} %copy-done, bf16[4096,768]{1,0:T(8,128)(2,1)} %x_ref.3), custom_call_target="tpu_custom_call" | custom-call | flops 2000000000 | bytes 7000000 | tf_op jit(solution)/shard_map/own_margins/pallas_call | solution.py:274
  117.5 36.6 %collective-permute-done.6.meta = s32[8,256]{1,0:T(8,128)S(1)} collective-permute-done((s32[8,256]{1,0:T(8,128)S(1)}, s32[8,256]{1,0:T(8,128)S(1)}, u32[]{:S(2)}, u32[]{:S(2)}) %collective-permute-start.6) | collective-permute-done | bytes 8224 | tf_op jit(solution)/shard_map/ppermute | solution.py:18
  154.1 2.5 %second_slots.1 = (bf16[7168,768]{1,0:T(8,128)(2,1)}, f32[56,128]{1,0:T(8,128)}, f32[16,128]{1,0:T(8,128)S(1)}, s32[8,128]{1,0:T(8,128)S(1)}, s32[8,2048]{1,0:T(8,128)S(1)}) custom-call(bf16[16,768]{1,0:T(8,128)(2,1)S(1)} %get-tuple-element.36.centres, f32[8,128]{1,0:T(8,128)S(1)} %get-tuple-element.37.shifts, ...), custom_call_target="tpu_custom_call", output_to_operand_aliasing={{0}: (6, {}), {1}: (7, {})} | custom-call | flops 3000000000 | bytes 6000000 | tf_op jit(solution)/shard_map/second_slots/pallas_call | solution.py:346
  156.5 0.0 collective-permute-done.9.refs_3_
  156.6 0.0 collective-permute-done.8.refs_2_
  156.6 6.1 %first_slots.1 = (bf16[7168,768]{1,0:T(8,128)(2,1)}, f32[48,128]{1,0:T(8,128)}, f32[56,128]{1,0:T(8,128)}) custom-call(s32[8,128]{1,0:T(8,128)S(1)} %get-tuple-element.41.start, bf16[16,768]{1,0:T(8,128)(2,1)S(1)} %get-tuple-element.36.centres, f32[8,128]{1,0:T(8,128)S(1)} %get-tuple-element.37.shifts, ...), custom_call_target="tpu_custom_call", output_to_operand_aliasing={{0}: (9, {}), {1}: (10, {}), {2}: (11, {})} | custom-call | flops 3000000000 | bytes 7000000 | tf_op jit(solution)/shard_map/first_slots/pallas_call | solution.py:434
  (3 shorter events, 0.0 us)
Async XLA Ops:
  0.7 0.8 copy-start
  10.3 57.2 %collective-permute-start.1 = (bf16[528,768]{1,0:T(8,128)(2,1)S(1)}, bf16[528,768]{1,0:T(8,128)(2,1)S(1)}, u32[]{:S(2)}, u32[]{:S(2)}) collective-permute-start(bf16[528,768]{1,0:T(8,128)(2,1)S(1)} %get-tuple-element.30.extra.own), channel_id=1, source_target_pairs={{0,16},{1,17},{2,18},{3,19},{4,20},{5,21},{6,22},{7,23},{8,24},{9,... | collective-permute-start | bytes 2433032 | tf_op jit(solution)/shard_map/ppermute | solution.py:18
  14.4 69.2 %collective-permute-start.7 = (bf16[512,768]{1,0:T(8,128)(2,1)S(1)}, bf16[512,768]{1,0:T(8,128)(2,1)S(1)}, u32[]{:S(2)}, u32[]{:S(2)}) collective-permute-start(bf16[512,768]{1,0:T(8,128)(2,1)S(1)} %get-tuple-element.45), channel_id=1, source_target_pairs={{0,16},{1,17},{2,18},{3,19},{4,20},{5,21},{6,22},{7,23},{8,24},{9,... | collective-permute-start | bytes 2359304 | tf_op jit(solution)/shard_map/ppermute | solution.py:18
  29.5 57.1 %collective-permute-start = (bf16[528,768]{1,0:T(8,128)(2,1)S(1)}, bf16[528,768]{1,0:T(8,128)(2,1)S(1)}, u32[]{:S(2)}, u32[]{:S(2)}) collective-permute-start(bf16[528,768]{1,0:T(8,128)(2,1)S(1)} %get-tuple-element.33), channel_id=1, source_target_pairs={{0,8},{1,9},{2,10},{3,11},{4,12},{5,13},{6,14},{7,15},{8,0},{9,1},... | collective-permute-start | bytes 2433032 | tf_op jit(solution)/shard_map/ppermute | solution.py:18
  67.5 35.6 %collective-permute-start.2 = (bf16[528,768]{1,0:T(8,128)(2,1)S(1)}, bf16[528,768]{1,0:T(8,128)(2,1)S(1)}, u32[]{:S(2)}, u32[]{:S(2)}) collective-permute-start(bf16[528,768]{1,0:T(8,128)(2,1)S(1)} %collective-permute-done.1.b.first.refs_0_), channel_id=1, source_target_pairs={{0,8},{1,9},{2,10},{3,11},{4,12},{5,13},{6,14},{7,15},{8,0},{9,1},... | collective-permute-start | bytes 2433032 | tf_op jit(solution)/shard_map/ppermute | solution.py:18
  83.6 73.0 %collective-permute-start.9 = (bf16[512,768]{1,0:T(8,128)(2,1)S(1)}, bf16[512,768]{1,0:T(8,128)(2,1)S(1)}, u32[]{:S(2)}, u32[]{:S(2)}) collective-permute-start(bf16[512,768]{1,0:T(8,128)(2,1)S(1)} %get-tuple-element.48), channel_id=1, source_target_pairs={{0,16},{1,17},{2,18},{3,19},{4,20},{5,21},{6,22},{7,23},{8,24},{9,... | collective-permute-start | bytes 2359304 | tf_op jit(solution)/shard_map/ppermute | solution.py:18
  83.6 73.0 %collective-permute-start.8 = (bf16[512,768]{1,0:T(8,128)(2,1)S(1)}, bf16[512,768]{1,0:T(8,128)(2,1)S(1)}, u32[]{:S(2)}, u32[]{:S(2)}) collective-permute-start(bf16[512,768]{1,0:T(8,128)(2,1)S(1)} %get-tuple-element.47), channel_id=1, source_target_pairs={{0,16},{1,17},{2,18},{3,19},{4,20},{5,21},{6,22},{7,23},{8,24},{9,... | collective-permute-start | bytes 2359304 | tf_op jit(solution)/shard_map/ppermute | solution.py:18
  103.2 1.2 collective-permute-start.3
  104.4 3.8 %collective-permute-start.4 = (f32[8,768]{1,0:T(8,128)S(1)}, f32[8,768]{1,0:T(8,128)S(1)}, u32[]{:S(2)}, u32[]{:S(2)}) collective-permute-start(f32[8,768]{1,0:T(8,128)S(1)} %add.11), channel_id=1, source_target_pairs={{0,2},{1,3},{2,0},{3,1},{4,6},{5,7},{6,4},{7,5},{8,10},{9,11},{10,... | collective-permute-start | bytes 73736 | tf_op jit(solution)/shard_map/ppermute | solution.py:18
  108.2 3.8 %collective-permute-start.5 = (f32[8,768]{1,0:T(8,128)S(1)}, f32[8,768]{1,0:T(8,128)S(1)}, u32[]{:S(2)}, u32[]{:S(2)}) collective-permute-start(f32[8,768]{1,0:T(8,128)S(1)} %add.12), channel_id=1, source_target_pairs={{0,4},{1,5},{2,6},{3,7},{4,0},{5,1},{6,2},{7,3},{8,12},{9,13},{10,... | collective-permute-start | bytes 73736 | tf_op jit(solution)/shard_map/ppermute | solution.py:18
  110.0 44.1 %collective-permute-start.6 = (s32[8,256]{1,0:T(8,128)S(1)}, s32[8,256]{1,0:T(8,128)S(1)}, u32[]{:S(2)}, u32[]{:S(2)}) collective-permute-start(s32[8,256]{1,0:T(8,128)S(1)} %get-tuple-element.38), channel_id=1, source_target_pairs={{0,16},{1,17},{2,18},{3,19},{4,20},{5,21},{6,22},{7,23},{8,24},{9,... | collective-permute-start | bytes 24584 | tf_op jit(solution)/shard_map/ppermute | solution.py:18
